TPU v7x, 32 devices: a whole 2x2x4 slice. The times are simulated.
32 devices in a mesh: org: 4 (over x, core), dst: 8 (over z, y).
Axes of the slice: x: 2, y: 2, z: 4, core: 2. Of those that a mesh axis runs over, the one named last changes fastest.
Arguments:
- anchor_coords: float32 [2, 2048], P(None, 'org'), may hold values from 0 to 1
- dest_coords: float32 [2, 4096], P(None, 'dst'), may hold values from 0 to 1
- hour_decay: float32 [8], replicated, may hold values from 16 to 64
- anchor_district: int32 [2048], P('org'), may hold values from 0 to 511, as said below
- dest_district: int32 [4096], P('dst'), may hold values from 0 to 511, as said below
- anchor_target: float32 [8, 2048], P(None, 'org'), may hold values from 0.5 to 2
- dest_target: float32 [8, 4096], P(None, 'dst'), may hold values from 0.5 to 2
- pair_share: float32 [512, 512], replicated, may hold values from 0.5 to 2
- catchment: int32 [256, 512], P('org', 'dst'), may hold values from 0 to 1023
Outputs:
- pair_factor: float32 [512, 512], replicated
- anchor_factor: float32 [8, 2048], P(None, 'org')
- dest_factor: float32 [8, 4096], P(None, 'dst')
- lane_flows: float32 [8, 1024], P(None, ('org', 'dst'))
Inputs may be any that keep to these rules, and one draw needn't show every extreme that they name: `anchor_district`: every district holds exactly 4 anchor zones. `dest_district`: every district holds exactly 8 destination zones.
All inputs are finite; a program needn't handle non-finite values.
Results may differ from a plain program's by a relative error of at most 0.00012.
Values sent between devices are 32-bit elements; how exact they have to be, the bound alone decides.
A program may use at most 128 MiB of HBM per device.

v0:
```python
import jax
import jax.numpy as jnp
from jax import lax
from jax.sharding import PartitionSpec as P

TB = 8
LANE_DEV = 32
SWEEPS = 2


def per_device(
    anchor_coords,
    dest_coords,
    hour_decay,
    anchor_district,
    dest_district,
    anchor_target,
    dest_target,
    pair_share,
    catchment,
):
    highest = lax.Precision.HIGHEST
    org_count = lax.axis_size("org")
    dst_count = lax.axis_size("dst")
    hours = hour_decay.shape[0]
    districts = pair_share.shape[0]
    org_rows = anchor_coords.shape[1]
    dst_cols = dest_coords.shape[1]
    flow_scale = org_rows * org_count * hours / (districts * districts)

    def onehot_of(ids, width):
        levels = jnp.arange(width, dtype=jnp.int32)
        return (ids[:, None] == levels[None, :]).astype(jnp.float32)

    def spread_of(factor, left, right):
        widened = jnp.dot(left, factor, precision=highest)
        return jnp.dot(widened, right.T, precision=highest)

    zone_left = onehot_of(anchor_district, districts)
    zone_right = onehot_of(dest_district, districts)
    row_coords, row_target, col_coords, col_target = (
        anchor_coords,
        anchor_target,
        dest_coords,
        dest_target,
    )
    left, right = (zone_left, zone_right)
    pair_factor = jnp.ones((districts, districts), jnp.float32)
    sq_distance = (row_coords[0][:, None] - col_coords[0][None, :]) ** 2 + (
        row_coords[1][:, None] - col_coords[1][None, :]
    ) ** 2
    seed = jnp.exp(-hour_decay[:, None, None] * sq_distance[None, :, :])
    dest_factor = jnp.ones((hours, dst_cols), jnp.float32)
    anchor_factor = jnp.ones((hours, org_rows), jnp.float32)
    for sweep_index in range(SWEEPS):
        spread = spread_of(pair_factor, left, right)
        row_sums = jnp.stack(
            [
                jnp.sum(seed[hour] * spread * dest_factor[hour][None, :], axis=1)
                for hour in range(hours)
            ]
        )
        anchor_factor = row_target / lax.psum(row_sums, "dst")
        col_sums = jnp.stack(
            [
                jnp.sum(anchor_factor[hour][:, None] * seed[hour] * spread, axis=0)
                for hour in range(hours)
            ]
        )
        dest_factor = col_target / lax.psum(col_sums, "org")
        weight = jnp.zeros((org_rows, dst_cols), jnp.float32)
        for hour in range(hours):
            weight = weight + anchor_factor[hour][:, None] * seed[hour] * dest_factor[hour][None, :]
        by_anchor = jnp.dot(left.T, weight, precision=highest)
        partial_value = jnp.dot(by_anchor, right, precision=highest)
        totals = lax.psum(partial_value, ("org", "dst"))
        pair_factor = pair_share * flow_scale / totals
    spread = spread_of(pair_factor, zone_left, zone_right)
    tile_list = []
    for hour in range(hours):
        flows = anchor_factor[hour][:, None] * seed[hour] * dest_factor[hour][None, :] * spread
        tile_list.append(
            flows.reshape(org_rows // TB, TB, dst_cols // TB, TB).sum(axis=(1, 3)).reshape(-1)
        )
    tile_sums = jnp.stack(tile_list)
    lane_count = LANE_DEV * org_count * dst_count
    partial_lanes = jax.ops.segment_sum(tile_sums.T, catchment.reshape(-1), lane_count).T
    lanes_out = lax.psum_scatter(partial_lanes, ("org", "dst"), scatter_dimension=1, tiled=True)
    return (pair_factor, anchor_factor, dest_factor, lanes_out)


def solution(mesh):
    return jax.shard_map(
        per_device,
        mesh=mesh,
        in_specs=(
            P(None, "org"),
            P(None, "dst"),
            P(),
            P("org"),
            P("dst"),
            P(None, "org"),
            P(None, "dst"),
            P(),
            P("org", "dst"),
        ),
        out_specs=(P(), P(None, "org"), P(None, "dst"), P(None, ("org", "dst"))),
        check_vma=False,
    )
```

profile of v0, /device:TPU:0, one launch (start us, length us, event | category | flops | bytes accessed | tf_op | source)
XLA Modules:
  0.0 726.6 jit_solution(14008893240605845730)
XLA Ops:
  13.1 3.2 copy-done
  16.3 3.5 multiply_reduce_fusion.24
  19.9 38.8 %psum.42 = f32[8,512]{1,0:T(8,128)S(1)} all-reduce(f32[8,512]{1,0:T(8,128)S(1)} %stack.119), channel_id=1, replica_groups=mesh['org'=4,'dst'=8] {'dst'}, use_global_device_ids=true, to_apply=%region_8.0 | all-reduce | flops 4096 | bytes 32768 | tf_op jit(solution)/shard_map/psum | solution.py:63
  58.8 3.9 multiply_reduce_fusion.16
  62.8 10.2 %psum.43 = f32[8,512]{1,0:T(8,128)S(1)} all-reduce(f32[8,512]{1,0:T(8,128)S(1)} %stack.128), channel_id=1, replica_groups=mesh['org'=4,'dst'=8] {'org'}, use_global_device_ids=true, to_apply=%region_17.0 | all-reduce | flops 4096 | bytes 32768 | tf_op jit(solution)/shard_map/psum | solution.py:70
  73.1 5.0 fusion.10
  80.3 127.3 %all-reduce.3.cloned.1.call-done = f32[512,512]{1,0:T(8,128)} async-done(((f32[512,512]{1,0:T(8,128)}), f32[512,512]{1,0:T(8,128)}) %all-reduce.3.cloned.1.call-update) | async-done | bytes 1048592 | tf_op jit(solution)/shard_map/psum | solution.py:76
  210.1 5.7 multiply_reduce_fusion.8
  215.9 36.4 %psum.45 = f32[8,512]{1,0:T(8,128)S(1)} all-reduce(f32[8,512]{1,0:T(8,128)S(1)} %stack.137), channel_id=1, replica_groups=mesh['org'=4,'dst'=8] {'dst'}, use_global_device_ids=true, to_apply=%region_27.0 | all-reduce | flops 4096 | bytes 32768 | tf_op jit(solution)/shard_map/psum | solution.py:63
  252.3 3.9 multiply_reduce_fusion
  256.3 10.4 %psum.46 = f32[8,512]{1,0:T(8,128)S(1)} all-reduce(f32[8,512]{1,0:T(8,128)S(1)} %stack.146), channel_id=1, replica_groups=mesh['org'=4,'dst'=8] {'org'}, use_global_device_ids=true, to_apply=%region_36.0 | all-reduce | flops 4096 | bytes 32768 | tf_op jit(solution)/shard_map/psum | solution.py:70
  266.7 5.0 fusion
  274.0 126.1 %all-reduce.5.cloned.1.call-done = f32[512,512]{1,0:T(8,128)} async-done(((f32[512,512]{1,0:T(8,128)}), f32[512,512]{1,0:T(8,128)}) %all-reduce.5.cloned.1.call-update) | async-done | bytes 1048592 | tf_op jit(solution)/shard_map/psum | solution.py:76
  406.5 4.7 multiply_multiply_fusion
  411.2 12.0 %reshape.117 = f32[64,8,64,8]{3,2,1,0:T(8,128)} reshape(f32[512,512]{1,0:T(8,128)} %get-tuple-element.49) | data formatting | bytes 2097152 | tf_op jit(solution)/shard_map/reshape | solution.py:83
  423.3 7.0 reduce_sum.394
  430.3 12.0 %reshape.118 = f32[64,8,64,8]{3,2,1,0:T(8,128)} reshape(f32[512,512]{1,0:T(8,128)} %get-tuple-element.48) | data formatting | bytes 2097152 | tf_op jit(solution)/shard_map/reshape | solution.py:83
  442.4 7.0 reduce_sum.395
  449.4 12.0 %reshape.119 = f32[64,8,64,8]{3,2,1,0:T(8,128)} reshape(f32[512,512]{1,0:T(8,128)} %get-tuple-element.47) | data formatting | bytes 2097152 | tf_op jit(solution)/shard_map/reshape | solution.py:83
  461.5 7.0 reduce_sum.396
  468.5 12.0 %reshape.120 = f32[64,8,64,8]{3,2,1,0:T(8,128)} reshape(f32[512,512]{1,0:T(8,128)} %get-tuple-element.46) | data formatting | bytes 2097152 | tf_op jit(solution)/shard_map/reshape | solution.py:83
  480.6 7.0 reduce_sum.397
  487.6 12.0 %reshape.121 = f32[64,8,64,8]{3,2,1,0:T(8,128)} reshape(f32[512,512]{1,0:T(8,128)} %get-tuple-element.45) | data formatting | bytes 2097152 | tf_op jit(solution)/shard_map/reshape | solution.py:83
  499.7 7.0 reduce_sum.398
  506.7 11.3 %reshape.122 = f32[64,8,64,8]{3,2,1,0:T(8,128)} reshape(f32[512,512]{1,0:T(8,128)S(1)} %get-tuple-element.44) | data formatting | bytes 2097152 | tf_op jit(solution)/shard_map/reshape | solution.py:83
  518.0 7.0 reduce_sum.399
  525.0 11.2 %reshape.115 = f32[64,8,64,8]{3,2,1,0:T(8,128)} reshape(f32[512,512]{1,0:T(8,128)S(1)} %get-tuple-element.51) | data formatting | bytes 2097152 | tf_op jit(solution)/shard_map/reshape | solution.py:83
  536.2 7.0 reduce_sum.392
  543.3 11.2 %reshape.116 = f32[64,8,64,8]{3,2,1,0:T(8,128)} reshape(f32[512,512]{1,0:T(8,128)S(1)} %get-tuple-element.50) | data formatting | bytes 2097152 | tf_op jit(solution)/shard_map/reshape | solution.py:83
  554.4 7.0 reduce_sum.393
  562.3 23.1 %scatter_custom_fusion = f32[1024,8]{1,0:T(8,128)} fusion(s32[4096]{0:T(1024)S(1)} %reshape.125, f32[4096,8]{1,0:T(8,128)S(1)} %copy.14, f32[]{:T(128)} %constant.1.clone.1), kind=kCustom, calls=%fused_computation.156 | custom fusion | flops 32768 | bytes 32772 | tf_op jit(solution)/shard_map/scatter-add | solution.py:87
  585.4 133.1 %reduce-scatter.2.cloned.1.call-done = f32[8,32]{0,1:T(8,128)} async-done(((f32[8,1024]{0,1:T(8,128)}), f32[8,32]{0,1:T(8,128)}) %reduce-scatter.2.cloned.1.call-update) | async-done | bytes 1040 | tf_op jit(solution)/shard_map/reduce_scatter | solution.py:88
  (61 shorter events, 22.3 us)
Async XLA Ops:
  7.2 9.2 %copy-start.8 = (s32[512]{0:T(512)S(1)}, s32[512]{0:T(512)}, u32[]{:S(2)}) copy-start(s32[512]{0:T(512)} %param.13) | copy-start | bytes 6148
  7.2 200.5 %all-reduce.3.cloned.1.call-start = ((), (), s32[]{:S(2)}) async-start(), calls=%async_computation.1 | async-start | bytes 2097152 | tf_op jit(solution)/shard_map/psum | solution.py:76
  11.4 47.4 %copy-start.3 = (f32[8,512]{1,0:T(8,128)S(1)}, f32[8,512]{1,0:T(8,128)}, u32[]{:S(2)}) copy-start(f32[8,512]{1,0:T(8,128)} %param.14) | copy-start | bytes 49156
  13.1 3.2 copy-start
  16.3 56.7 %copy-start.4 = (f32[8,512]{1,0:T(8,128)S(1)}, f32[8,512]{1,0:T(8,128)}, u32[]{:S(2)}) copy-start(f32[8,512]{1,0:T(8,128)} %param.15) | copy-start | bytes 49156
  16.3 56.8 %copy-start.9 = (s32[512]{0:T(512)S(1)}, s32[512]{0:T(512)}, u32[]{:S(2)}) copy-start(s32[512]{0:T(512)} %param.12) | copy-start | bytes 6148
  62.8 144.9 %copy-start.2 = (f32[512,512]{1,0:T(8,128)S(1)}, f32[512,512]{1,0:T(8,128)}, u32[]{:S(2)}) copy-start(f32[512,512]{1,0:T(8,128)} %param.16) | copy-start | bytes 3145732
  80.3 319.8 %all-reduce.5.cloned.1.call-start = ((), (), s32[]{:S(2)}) async-start(), calls=%async_computation.2 | async-start | bytes 2097152 | tf_op jit(solution)/shard_map/psum | solution.py:76
  252.3 19.5 %copy-start.5 = (f32[8,512]{1,0:T(8,128)}, f32[8,512]{1,0:T(8,128)S(1)}, u32[]{:S(2)}) copy-start(f32[8,512]{1,0:T(8,128)S(1)} %div.21) | copy-start | bytes 49156
  256.2 17.7 %copy-start.7 = (s32[64,64]{1,0:T(8,128)S(1)}, s32[64,64]{1,0:T(8,128)}, u32[]{:S(2)}) copy-start(s32[64,64]{1,0:T(8,128)} %param.17) | copy-start | bytes 49156
  266.7 137.0 %copy-start.6 = (f32[8,512]{1,0:T(8,128)}, f32[8,512]{1,0:T(8,128)S(1)}, u32[]{:S(2)}) copy-start(f32[8,512]{1,0:T(8,128)S(1)} %div.22) | copy-start | bytes 49156
  273.9 444.6 %reduce-scatter.2.cloned.1.call-start = ((), (), s32[]{:S(2)}) async-start(), calls=%async_computation.3 | async-start | bytes 540672 | tf_op jit(solution)/shard_map/reduce_scatter | solution.py:88
  401.6 1.0 copy-start.1
Sparse Core Ops, SparseCore 0:
  80.4 127.2 all-reduce.2
  274.0 126.0 all-reduce.4
  585.5 132.9 reduce-scatter.1
where the time goes:
time: 741 us; the launch traced here: 727 us
  waiting for transfers between devices  387 us (52%)
  local copies, waits for them, and re-layouts  103 us (14%)
  blocking collectives  95.8 us (13%)
  other arithmetic  95.5 us (13%)
  matrix products  31.6 us (4%)
  between operations  14.2 us (2%)
    psum x2, waiting for transfers between devices, per_device(): totals = lax.psum(partial_value, ('org', 'dst'))  253 us
    reduce_scatter x1, waiting for transfers between devices, per_device(): lax.psum_scatter(partial_lanes, ('org', 'dst'), scatter_dimension=1, tile...  133 us
    reshape x8, local copies, waits for them, and re-layouts, per_device(): flows.reshape(org_rows // TB, TB, dst_cols // TB, TB).sum(axis=(1, 3))  93.9 us
    psum x2, blocking collectives, per_device(): anchor_factor = row_target / lax.psum(row_sums, 'dst')  75.2 us
    reduce_sum x8, other arithmetic, per_device(): flows.reshape(org_rows // TB, TB, dst_cols // TB, TB).sum(axis=(1, 3))  55.6 us
    scatter-add x1, other arithmetic, per_device(): jax.ops.segment_sum(tile_sums.T, catchment.reshape(-1), lane_count)  23.1 us
    psum x2, blocking collectives, per_device(): dest_factor = col_target / lax.psum(col_sums, 'org')  20.6 us
  transfers between devices with their start and end apart: 3, of which 3 were waited for; matrix products, arithmetic and copies ran while one was open for 0% of the time, Pallas kernels for 0%

commit v1 on v0

v1 whole, which is shorter than its diff:
```python
import functools

import jax
import jax.numpy as jnp
from jax import lax
from jax.experimental import pallas as pl
from jax.experimental.pallas import tpu as pltpu
from jax.sharding import PartitionSpec as P

TB = 8
LANE_DEV = 32
SWEEPS = 2
CH = 32
F32 = jnp.float32
BF16 = jnp.bfloat16


def nn(a, b):
    return lax.dot_general(a, b, (((1,), (0,)), ((), ())), preferred_element_type=F32)


def nt(a, b):
    return lax.dot_general(a, b, (((1,), (1,)), ((), ())), preferred_element_type=F32)


def split(x, parts):
    out = []
    for _ in range(parts):
        top = x.astype(BF16)
        out.append(top)
        x = x - top.astype(F32)
    return out


def iota(shape, axis):
    return lax.broadcasted_iota(jnp.int32, shape, axis)


def onehot(mask):
    return jnp.where(mask, 1.0, 0.0).astype(BF16)


def kernel(
    A, B, decay_ref, ac_ref, dc_ref, ad_ref, dd_ref, at_ref, dt_ref, share_ref, catch_ref,
    pf_out, a_out, b_out, lane_out,
    fa, fd, ta, td, pa, pd, seed, acc, u, spread, acol, colacc, rsum, csum,
    rbuf, cbuf, asnd, bsnd, abuf, bbuf, pfb, full, tsum, lanes, lbuf, lsum, mbuf,
    s_fa, r_fa, s_fd, r_fd, s_ta, r_ta, s_td, r_td, s_row, r_row, s_col, r_col,
    s_a, r_a, s_b, r_b, s_p1, r_p1, s_px, r_px, s_pc, r_pc, s_l, r_l, s_m, r_m,
):
    i = lax.axis_index("org")
    j = lax.axis_index("dst")
    N = ac_ref.shape[1]
    hours = at_ref.shape[0]
    districts = share_ref.shape[0]
    gd = districts // A
    kd = districts // B
    ra = N // gd
    rd = N // kd
    pack = 128 // kd
    scale = N * A * hours / (districts * districts)

    def remote(src, dst, ssem, rsem, org, dst_at):
        return pltpu.make_async_remote_copy(
            src_ref=src, dst_ref=dst, send_sem=ssem, recv_sem=rsem,
            device_id=(org, dst_at), device_id_type=pl.DeviceIdType.MESH)

    def exchange(axis, src_of, buf, ssem, rsem):
        me, n = (i, A) if axis == "org" else (j, B)
        sends = []
        for k in range(1, n):
            peer = lax.rem(me + k, n)
            dev = (peer, j) if axis == "org" else (i, peer)
            c = remote(src_of(peer), buf.at[me], ssem.at[k - 1], rsem.at[me], *dev)
            c.start()
            sends.append(c)

        def finish():
            for k in range(1, n):
                peer = lax.rem(me + k, n)
                dev = (peer, j) if axis == "org" else (i, peer)
                remote(buf.at[peer], buf.at[peer], ssem.at[k - 1], rsem.at[peer], *dev).wait_recv()
            for c in sends:
                c.wait_send()

        return finish

    def gathered(axis, value, buf, ssem, rsem):
        me = i if axis == "org" else j
        buf[me] = value
        return exchange(axis, lambda peer: buf.at[me], buf, ssem, rsem)

    def summed(buf, n):
        total = buf[0]
        for q in range(1, n):
            total = total + buf[q]
        return total

    barrier = pltpu.get_barrier_semaphore()
    for k in range(1, A):
        pl.semaphore_signal(barrier, inc=1, device_id=(lax.rem(i + k, A), j),
                            device_id_type=pl.DeviceIdType.MESH)
    for k in range(1, B):
        pl.semaphore_signal(barrier, inc=1, device_id=(i, lax.rem(j + k, B)),
                            device_id_type=pl.DeviceIdType.MESH)
    pl.semaphore_wait(barrier, A + B - 2)

    pad = jnp.zeros((5, N), F32)
    geo_a = jnp.concatenate([ac_ref[...], ad_ref[...].astype(F32), pad], axis=0)
    geo_d = jnp.concatenate([dc_ref[...], dd_ref[...].astype(F32), pad], axis=0)
    end_fd = gathered("dst", geo_d, fd, s_fd, r_fd)
    end_fa = gathered("org", geo_a, fa, s_fa, r_fa)
    end_td = gathered("dst", dt_ref[...], td, s_td, r_td)
    end_ta = gathered("org", at_ref[...], ta, s_ta, r_ta)

    before = onehot(iota((N, N), 0) < iota((N, N), 1))

    def place(feats, table, n, me, width, ranks):
        carry = jnp.zeros((width, 1), F32)
        for q in range(n):
            ids = feats[q, 2:3, :].astype(jnp.int32) - me * width
            mine = iota((width, N), 0) == ids
            flag = jnp.where(mine, 1.0, 0.0)
            count = nn(flag.astype(BF16), before) + carry
            carry = carry + jnp.sum(flag, axis=1, keepdims=True)
            for r in range(ranks):
                table[q, r * width:(r + 1) * width, :] = jnp.where(
                    count == r, flag, 0.0).astype(BF16)

    end_fa()
    place(fa, pa, A, i, gd, ra)
    acol_geo = jnp.zeros((N, 8), F32)
    for q in range(A):
        for part in split(fa[q], 3):
            acol_geo = acol_geo + nt(pa[q], part)
    acol[:, 0:8] = acol_geo
    end_fd()
    place(fd, pd, B, j, kd, rd)
    drow = jnp.zeros((8, N), F32)
    for q in range(B):
        for part in split(fd[q], 3):
            drow = drow + nt(part, pd[q])
    dx, dy = drow[0:1, :], drow[1:2, :]

    def fold(x):
        y = x[:, 0:128]
        for q in range(1, N // 128):
            y = y + x[:, q * 128:(q + 1) * 128]
        return y

    def seed_body(c, _):
        rows = pl.ds(pl.multiple_of(c * CH, CH), CH)
        xy = acol[rows, :]
        sq = (xy[:, 0:1] - dx) ** 2 + (xy[:, 1:2] - dy) ** 2
        for h in range(hours):
            s = jnp.exp(-decay_ref[h] * sq)
            seed[h, rows, :] = s
            acc[h, rows, :] = fold(s)
        return 0

    lax.fori_loop(0, N // CH, seed_body, 0)

    end_ta()
    end_td()
    a_target = jnp.zeros((8, N), F32)
    for q in range(A):
        for part in split(ta[q], 3):
            a_target = a_target + nt(part, pa[q])
    d_target = jnp.zeros((8, N), F32)
    for q in range(B):
        for part in split(td[q], 3):
            d_target = d_target + nt(part, pd[q])
    rsum[...] = a_target
    csum[...] = d_target

    eye = onehot(iota((N, N), 0) == iota((N, N), 1))
    pieces = []
    for q in range(pack):
        pieces.append(None)
    at_lane = pl.multiple_of(lax.div(j, pack) * 128, 128)
    wide = share_ref[pl.ds(pl.multiple_of(i * gd, gd), gd), pl.ds(at_lane, 128)]
    share = wide[:, 0:kd]
    for q in range(1, pack):
        share = jnp.where(lax.rem(j, pack) == q, wide[:, q * kd:(q + 1) * kd], share)

    dest = None
    for sweep in range(SWEEPS):
        if sweep > 0:
            def row_body(q, _):
                at = pl.multiple_of(q * CH, CH)
                sp = spread[pl.ds(at, CH), :]
                for h in range(hours):
                    sb = sp * dest[h:h + 1, :]
                    for r in range(ra):
                        rows = pl.ds(at + r * gd, CH)
                        acc[h, rows, :] = fold(seed[h, rows, :] * sb)
                return 0

            lax.fori_loop(0, gd // CH, row_body, 0)
        rows_sum = jnp.zeros((8, N), F32)
        for h in range(hours):
            pick = onehot(iota((8, 128), 0) == h)
            for part in split(acc[h], 2):
                rows_sum = rows_sum + nt(pick, part)
        gathered("dst", rows_sum, rbuf.at[sweep], s_row.at[sweep], r_row.at[sweep])()
        anchor = rsum[...] / summed(rbuf.at[sweep], B)
        parts = split(anchor, 3)
        acol[:, 0:8] = nt(eye, parts[0]) + nt(eye, parts[1]) + nt(eye, parts[2])
        if sweep == SWEEPS - 1:
            for q in range(A):
                asnd[q] = nn(parts[0], pa[q]) + nn(parts[1], pa[q]) + nn(parts[2], pa[q])
            abuf[i] = asnd[i]
            end_a = exchange("org", lambda peer: asnd.at[peer], abuf, s_a, r_a)
        colacc[...] = jnp.zeros_like(colacc)

        def col_body(q, _):
            at = pl.multiple_of(q * CH, CH)
            for h in range(hours):
                t = None
                for r in range(ra):
                    rows = pl.ds(at + r * gd, CH)
                    term = acol[rows, h:h + 1] * seed[h, rows, :]
                    t = term if t is None else t + term
                u[h, pl.ds(at, CH), :] = t
                if sweep > 0:
                    t = t * spread[pl.ds(at, CH), :]
                colacc[h] = colacc[h] + jnp.sum(t.reshape(CH // 8, 8, N), axis=0)
            return 0

        lax.fori_loop(0, gd // CH, col_body, 0)
        cols_sum = jnp.concatenate(
            [jnp.sum(colacc[h], axis=0, keepdims=True) for h in range(hours)], axis=0)
        gathered("org", cols_sum, cbuf.at[sweep], s_col.at[sweep], r_col.at[sweep])()
        dest = csum[...] / summed(cbuf.at[sweep], A)
        if sweep == SWEEPS - 1:
            parts = split(dest, 3)
            for q in range(B):
                bsnd[q] = nn(parts[0], pd[q]) + nn(parts[1], pd[q]) + nn(parts[2], pd[q])
            bbuf[j] = bsnd[j]
            end_b = exchange("dst", lambda peer: bsnd.at[peer], bbuf, s_b, r_b)

        def total_body(q, _):
            rows = pl.ds(pl.multiple_of(q * CH, CH), CH)
            t = u[0, rows, :] * dest[0:1, :]
            for h in range(1, hours):
                t = t + u[h, rows, :] * dest[h:h + 1, :]
            acc[0, rows, :] = fold(t)
            return 0

        lax.fori_loop(0, gd // CH, total_body, 0)
        folded = acc[0, 0:gd, :]
        totals = folded[:, 0:kd]
        for q in range(1, pack):
            totals = totals + folded[:, q * kd:(q + 1) * kd]
        pair = share * scale / totals
        if sweep < SWEEPS - 1:
            spread[...] = jnp.concatenate([pair] * rd, axis=1)

    ph = gd // pack
    pfb[i, j] = jnp.concatenate([pair[q * ph:(q + 1) * ph, :] for q in range(pack)], axis=1)
    core = lax.rem(i, 2)
    X = A // 2
    sib = i + 1 - 2 * core
    pending = []
    for k in range(1, B):
        c = remote(pfb.at[i, j], pfb.at[i, j], s_p1.at[k - 1], r_p1.at[j], i, lax.rem(j + k, B))
        c.start()
        pending.append(c)

    def spread_x(b):
        for k in range(1, X):
            to = lax.rem(i + 2 * k, A)
            c = remote(pfb.at[i, b], pfb.at[i, b], s_px.at[k - 1, b], r_px.at[k - 1, b], to, j)
            c.start()
            pending.append(c)

    def to_core(g, b, slot):
        c = remote(pfb.at[g, b], pfb.at[g, b], s_pc.at[slot, b], r_pc.at[slot, b], sib, j)
        c.start()
        pending.append(c)

    spread_x(j)
    to_core(i, j, 0)

    o = iota((N, N), 0)
    half = N // TB // 2
    r_of = lax.div(o, 2 * half)
    e_of = lax.rem(lax.div(o, half), 2)
    p_of = lax.rem(o, half)
    order = onehot(iota((N, N), 1) == (2 * p_of + e_of) * TB + r_of)
    own = jnp.zeros((N, 8), F32)
    for part in split(geo_a, 3):
        own = own + nt(order, part)
    end_a()
    end_b()
    a_own = summed(abuf, A)
    b_own = summed(bbuf, B)
    a_out[...] = a_own
    b_out[...] = b_own
    parts = split(a_own, 3)
    acol[:, 0:8] = nt(order, parts[0]) + nt(order, parts[1]) + nt(order, parts[2])
    acol[:, 8:16] = own
    ex, ey = dc_ref[0:1, :], dc_ref[1:2, :]

    def flow_body(c, _):
        rows = pl.ds(pl.multiple_of(c * CH, CH), CH)
        col = acol[rows, :]
        sq = (col[:, 8:9] - ex) ** 2 + (col[:, 9:10] - ey) ** 2
        for h in range(hours):
            seed[h, rows, :] = col[:, h:h + 1] * jnp.exp(-decay_ref[h] * sq) * b_own[h:h + 1, :]
        return 0

    def recv(g, b, sem):
        remote(pfb.at[g, b], pfb.at[g, b], s_p1.at[0], sem, sib, j).wait_recv()

    steps = N // CH
    lax.fori_loop(0, steps // 2, flow_body, 0)
    for k in range(1, B):
        b = lax.rem(j + k, B)
        recv(i, b, r_p1.at[b])
        spread_x(b)
        to_core(i, b, 0)
    lax.fori_loop(steps // 2, steps, flow_body, 0)
    for k in range(1, X):
        g = lax.rem(i + A - 2 * k, A)
        for m in range(B):
            b = lax.rem(j + m, B)
            recv(g, b, r_px.at[k - 1, b])
            to_core(g, b, k)
    left = onehot(own[:, 2:3].astype(jnp.int32) == iota((N, districts), 1))
    right = onehot(iota((districts, N), 0) == dd_ref[...])
    for k in range(X):
        g = lax.rem(sib + A - 2 * k, A)
        for m in range(B):
            b = lax.rem(j + m, B)
            recv(g, b, r_pc.at[k, b])
    for c in pending:
        c.wait_send()

    for g in range(A):
        for q in range(pack):
            full[g * gd + q * ph:g * gd + (q + 1) * ph, :] = jnp.concatenate(
                [pfb[g, b, :, q * kd:(q + 1) * kd] for b in range(B)], axis=1)
    pf_out[...] = full[...]
    high, low = split(full[...], 2)
    full[...] = nn(nn(left, high).astype(BF16), right) + nn(nn(left, low).astype(BF16), right)

    tiles = N // TB

    def tile_body(c, _):
        at = pl.multiple_of(c * 16, 16)
        for h in range(hours):
            t = None
            for r in range(TB):
                rows = pl.ds(at + r * tiles, 16)
                term = seed[h, rows, :] * full[rows, :]
                t = term if t is None else t + term
            acc[h, pl.ds(at, 16), :] = t[:, 0:128]
            for q in range(1, N // 128):
                acc[h, pl.ds(at + q * tiles, 16), :] = t[:, q * 128:(q + 1) * 128]
        return 0

    lax.fori_loop(0, tiles // 16, tile_body, 0)
    for h in range(hours):
        pair_sum = jnp.zeros((half, 128), F32)
        for q in range(N // 128):
            for e in range(2):
                at = q * tiles + e * half
                pool = onehot(lax.div(iota((128, 128), 0), TB) + q * (128 // TB) + e * tiles
                              == iota((128, 128), 1))
                for part in split(acc[h, at:at + half, :], 2):
                    pair_sum = pair_sum + nn(part, pool)
        tsum[h] = pair_sum

    slabs = lanes.shape[0]
    result = jnp.zeros((slabs * 8, 128), F32)
    slab_of = lax.div(iota((slabs * 8, 128), 0), 8)
    for p in range(half):
        ids = catch_ref[p:p + 1, :]
        top = lax.div(ids, 128)
        low_of = ids - top * 128
        t = tsum[:, p, :]
        t = jnp.concatenate([t] * slabs, axis=0)
        t = jnp.where(slab_of == top, t, 0.0)
        lo = onehot(iota((128, 128), 0) == low_of)
        for part in split(t, 2):
            result = result + nt(part, lo)
    lanes[...] = result.reshape(slabs, 8, 128)

    per = slabs // A
    lbuf[i] = lanes[pl.ds(i * per, per)]
    exchange("org", lambda peer: lanes.at[pl.ds(peer * per, per)], lbuf, s_l, r_l)()
    lsum[...] = summed(lbuf, A)
    share_of = 128 // LANE_DEV
    mbuf[j] = lsum[lax.div(j, share_of)]
    exchange("dst", lambda peer: lsum.at[lax.div(peer, share_of)], mbuf, s_m, r_m)()
    total = summed(mbuf, B)
    mine = total[:, 0:LANE_DEV]
    for q in range(1, share_of):
        mine = jnp.where(lax.rem(j, share_of) == q,
                         total[:, q * LANE_DEV:(q + 1) * LANE_DEV], mine)
    lane_out[...] = mine


def per_device(
    anchor_coords, dest_coords, hour_decay, anchor_district, dest_district,
    anchor_target, dest_target, pair_share, catchment,
):
    A = lax.axis_size("org")
    B = lax.axis_size("dst")
    N = anchor_coords.shape[1]
    hours = hour_decay.shape[0]
    districts = pair_share.shape[0]
    gd, kd = districts // A, districts // B
    ph = gd // (128 // kd)
    slabs = LANE_DEV * A * B // 128
    V = pltpu.VMEM
    dma = pltpu.SemaphoreType.DMA
    scratch = [
        V((A, 8, N), F32), V((B, 8, N), F32), V((A, 8, N), F32), V((B, 8, N), F32),
        V((A, N, N), BF16), V((B, N, N), BF16),
        V((hours, N, N), F32), V((hours, N, 128), F32), V((hours, gd, N), F32),
        V((gd, N), F32), V((N, 128), F32), V((hours, 8, N), F32),
        V((8, N), F32), V((8, N), F32),
        V((SWEEPS, B, 8, N), F32), V((SWEEPS, A, 8, N), F32),
        V((A, 8, N), F32), V((B, 8, N), F32), V((A, 8, N), F32), V((B, 8, N), F32),
        V((A, B, ph, 128), F32), V((districts, districts), F32),
        V((hours, N // TB // 2, 128), F32), V((slabs, 8, 128), F32),
        V((A, slabs // A, 8, 128), F32), V((slabs // A, 8, 128), F32), V((B, 8, 128), F32),
    ]
    X = A // 2
    for shape in (
        (A,), (A,), (B,), (B,), (A,), (A,), (B,), (B,),
        (SWEEPS, B), (SWEEPS, B), (SWEEPS, A), (SWEEPS, A),
        (A,), (A,), (B,), (B,), (B,), (B,),
        (max(X - 1, 1), B), (max(X - 1, 1), B), (X, B), (X, B),
        (A,), (A,), (B,), (B,),
    ):
        scratch.append(dma(shape))
    vm = pl.BlockSpec(memory_space=pltpu.VMEM)
    return tuple(pl.pallas_call(
        functools.partial(kernel, A, B),
        out_shape=(
            jax.ShapeDtypeStruct((districts, districts), F32),
            jax.ShapeDtypeStruct((hours, N), F32),
            jax.ShapeDtypeStruct((hours, N), F32),
            jax.ShapeDtypeStruct((hours, LANE_DEV), F32),
        ),
        in_specs=[pl.BlockSpec(memory_space=pltpu.SMEM)] + [vm] * 8,
        out_specs=(vm, vm, vm, vm),
        scratch_shapes=scratch,
        compiler_params=pltpu.CompilerParams(
            collective_id=0, has_side_effects=True, vmem_limit_bytes=56 * 1024 * 1024),
    )(
        hour_decay, anchor_coords, dest_coords,
        anchor_district.reshape(1, N), dest_district.reshape(1, N),
        anchor_target, dest_target, pair_share,
        catchment.reshape(N // TB // 2, 128),
    ))


def solution(mesh):
    return jax.shard_map(
        per_device,
        mesh=mesh,
        in_specs=(
            P(None, "org"), P(None, "dst"), P(), P("org"), P("dst"),
            P(None, "org"), P(None, "dst"), P(), P("org", "dst"),
        ),
        out_specs=(P(), P(None, "org"), P(None, "dst"), P(None, ("org", "dst"))),
        check_vma=False,
    )
```

time: 741 us -> 98.4 us (0.13); the launches traced: 727 us -> 98.1 us
  waiting for transfers between devices: 387 us -> 0 us
  local copies, waits for them, and re-layouts: 103 us -> 5.7 us
  blocking collectives: 95.8 us -> 0 us
  other arithmetic: 95.5 us -> 0 us
  Pallas kernels: 0 us -> 91.8 us
  matrix products: 31.6 us -> 0 us
  between operations: 14.2 us -> 0.65 us
    psum x2 -> x0, waiting for transfers between devices: 253 us -> none  [per_device(): totals = lax.psum(partial_value, ('org', 'dst'))]
    reduce_scatter x1 -> x0, waiting for transfers between devices: 133 us -> none  [per_device(): lax.psum_scatter(partial_lanes, ('org', 'dst'), scatter_dimension=1, tile...]
    psum x4 -> x0, blocking collectives: 95.8 us -> none  [the longest x2 75.2 us: per_device(): anchor_factor = row_target / lax.psum(row_sums, 'dst')]
    reshape x8 -> x1, local copies, waits for them, and re-layouts: 93.9 us -> 1.43 us  [per_device(): catchment.reshape(N // TB // 2, 128)]
    pallas_call x0 -> x1, Pallas kernels: none -> 91.8 us  [per_device(): pl.pallas_call(functools.partial(kernel, A, B), out_shape=(jax.ShapeDtype...]
    reduce_sum x10 -> x0, other arithmetic: 63.5 us -> none  [the longest x8 55.6 us: per_device(): flows.reshape(org_rows // TB, TB, dst_cols // TB, TB).sum(axis=(1, 3))]
    dot_general x10 -> x0, matrix products: 31.6 us -> none  [the longest x3 12 us: spread_of(): return jnp.dot(widened, right.T, precision=highest)]
    scatter-add x1 -> x0, other arithmetic: 23.1 us -> none  [per_device(): jax.ops.segment_sum(tile_sums.T, catchment.reshape(-1), lane_count)]
  transfers between devices with their start and end apart: 3 -> 0, of which waited for: 3 -> 0; matrix products, arithmetic and copies ran while one was open for 0% -> 0% of each run, Pallas kernels for 0% -> 0%
where the time goes in v1:
time: 98.4 us; the launch traced here: 98.1 us
  Pallas kernels  91.8 us (93%)
  local copies, waits for them, and re-layouts  5.7 us (6%)
    pallas_call x1, Pallas kernels, per_device(): pl.pallas_call(functools.partial(kernel, A, B), out_shape=(jax.ShapeDtype...  91.8 us
    unnamed x10, local copies, waits for them, and re-layouts  4.26 us

profile of v1, /device:TPU:0, one launch (start us, length us, event | category | flops | bytes accessed | tf_op | source)
XLA Modules:
  0.0 98.1 jit_solution(1185113050779950282)
XLA Ops:
  0.6 1.4 %reshape.19.catch_ref = s32[32,128]{1,0:T(8,128)} reshape(s32[64,64]{1,0:T(8,128)} %param.17) | data formatting | bytes 32768 | tf_op jit(solution)/shard_map/reshape | solution.py:458
  2.1 91.8 %shard_map.120 = (f32[512,512]{1,0:T(8,128)}, f32[8,512]{1,0:T(8,128)}, f32[8,512]{1,0:T(8,128)}, f32[8,32]{1,0:T(8,128)}) custom-call(f32[8]{0:T(128)} %decay_ref.1, f32[2,512]{1,0:T(2,128)} %ac_ref.1, f32[2,512]{1,0:T(2,128)} %dc_ref.1, s32[1,512]{1,0:T(1,128)} %bitcast.2, s32[1,512]{1,0:T(1,128)} %bitcast.3, f32[8,512]{1,0:T(8,128)} %at_ref.1, ...), custom_call_target="tpu_custom_call" | custom-call | tf_op jit(solution)/shard_map/pallas_call | solution.py:441
  93.9 0.0 copy-start.1
  93.9 2.3 %copy.17 = f32[512,512]{1,0:T(8,128)} copy(f32[512,512]{1,0:T(8,128)} %get-tuple-element.8) | data formatting | bytes 2097152
  96.1 0.0 copy-done.1
  96.1 0.0 copy-start
  96.1 0.6 copy.18
  96.7 0.1 copy-done
  96.9 0.0 copy-start.2
  96.9 0.6 copy.19
  97.5 0.1 copy-done.2
  97.5 0.6 copy.20
Async XLA Ops:
  93.9 2.3 %copy-start.1 = (f32[8,512]{1,0:T(8,128)S(1)}, f32[8,512]{1,0:T(8,128)}, u32[]{:S(2)}) copy-start(f32[8,512]{1,0:T(8,128)} %get-tuple-element.9) | copy-start | bytes 49156
  96.1 0.7 copy-start
  96.9 0.7 copy-start.2

commit v2 on v1

--- a/solution.py
+++ b/solution.py
@@ -36,6 +36,18 @@
     return lax.broadcasted_iota(jnp.int32, shape, axis)
 
 
+def stacked(x, parts):
+    return jnp.concatenate([p.astype(F32) for p in split(x, parts)], axis=0).astype(BF16)
+
+
+def rows_added(y):
+    return y[0:8] + y[8:16] + y[16:24]
+
+
+def cols_added(y):
+    return y[:, 0:8] + y[:, 8:16] + y[:, 16:24]
+
+
 def onehot(mask):
     return jnp.where(mask, 1.0, 0.0).astype(BF16)
 
@@ -43,8 +55,9 @@
 def kernel(
     A, B, decay_ref, ac_ref, dc_ref, ad_ref, dd_ref, at_ref, dt_ref, share_ref, catch_ref,
     pf_out, a_out, b_out, lane_out,
-    fa, fd, ta, td, pa, pd, seed, acc, u, spread, acol, colacc, rsum, csum,
-    rbuf, cbuf, asnd, bsnd, abuf, bbuf, pfb, full, tsum, lanes, lbuf, lsum, mbuf,
+    fa, fd, ta, td, pa, pd, seed, acc, u, spread, acol, colacc,
+    rbuf, cbuf, asnd, bsnd, abuf, bbuf, pfb, full, mixed, tsum, lanes, lbuf, lsum, mbuf,
+    share_in, by_slab, by_low, s_share, s_pf,
     s_fa, r_fa, s_fd, r_fd, s_ta, r_ta, s_td, r_td, s_row, r_row, s_col, r_col,
     s_a, r_a, s_b, r_b, s_p1, r_p1, s_px, r_px, s_pc, r_pc, s_l, r_l, s_m, r_m,
 ):
@@ -96,6 +109,11 @@
             total = total + buf[q]
         return total
 
+    at_lane = pl.multiple_of(lax.div(j, pack) * 128, 128)
+    share_copy = pltpu.make_async_copy(
+        share_ref.at[pl.ds(pl.multiple_of(i * gd, gd), gd), pl.ds(at_lane, 128)],
+        share_in, s_share)
+    share_copy.start()
     barrier = pltpu.get_barrier_semaphore()
     for k in range(1, A):
         pl.semaphore_signal(barrier, inc=1, device_id=(lax.rem(i + k, A), j),
@@ -116,30 +134,35 @@
     before = onehot(iota((N, N), 0) < iota((N, N), 1))
 
     def place(feats, table, n, me, width, ranks):
+        flags = []
+        for q in range(n):
+            ids = feats[q, 2:3, :].astype(jnp.int32) - me * width
+            flags.append(jnp.where(iota((width, N), 0) == ids, 1.0, 0.0))
+        counts = nn(jnp.concatenate(flags, axis=0).astype(BF16), before)
         carry = jnp.zeros((width, 1), F32)
         for q in range(n):
-            ids = feats[q, 2:3, :].astype(jnp.int32) - me * width
-            mine = iota((width, N), 0) == ids
-            flag = jnp.where(mine, 1.0, 0.0)
-            count = nn(flag.astype(BF16), before) + carry
-            carry = carry + jnp.sum(flag, axis=1, keepdims=True)
+            flag = flags[q]
+            count = counts[q * width:(q + 1) * width, :] + carry
+            carry = count[:, N - 1:N] + flag[:, N - 1:N]
             for r in range(ranks):
                 table[q, r * width:(r + 1) * width, :] = jnp.where(
                     count == r, flag, 0.0).astype(BF16)
 
+    def to_slots(feats, table, n):
+        y = jnp.zeros((24, N), F32)
+        for q in range(n):
+            y = y + nt(stacked(feats[q], 3), table[q])
+        return rows_added(y)
+
     end_fa()
     place(fa, pa, A, i, gd, ra)
-    acol_geo = jnp.zeros((N, 8), F32)
+    geo = jnp.zeros((N, 24), F32)
     for q in range(A):
-        for part in split(fa[q], 3):
-            acol_geo = acol_geo + nt(pa[q], part)
-    acol[:, 0:8] = acol_geo
+        geo = geo + nt(pa[q], stacked(fa[q], 3))
+    acol[:, 0:8] = cols_added(geo)
     end_fd()
     place(fd, pd, B, j, kd, rd)
-    drow = jnp.zeros((8, N), F32)
-    for q in range(B):
-        for part in split(fd[q], 3):
-            drow = drow + nt(part, pd[q])
+    drow = to_slots(fd, pd, B)
     dx, dy = drow[0:1, :], drow[1:2, :]
 
     def fold(x):
@@ -160,30 +183,8 @@
 
     lax.fori_loop(0, N // CH, seed_body, 0)
 
-    end_ta()
-    end_td()
-    a_target = jnp.zeros((8, N), F32)
-    for q in range(A):
-        for part in split(ta[q], 3):
-            a_target = a_target + nt(part, pa[q])
-    d_target = jnp.zeros((8, N), F32)
-    for q in range(B):
-        for part in split(td[q], 3):
-            d_target = d_target + nt(part, pd[q])
-    rsum[...] = a_target
-    csum[...] = d_target
-
-    eye = onehot(iota((N, N), 0) == iota((N, N), 1))
-    pieces = []
-    for q in range(pack):
-        pieces.append(None)
-    at_lane = pl.multiple_of(lax.div(j, pack) * 128, 128)
-    wide = share_ref[pl.ds(pl.multiple_of(i * gd, gd), gd), pl.ds(at_lane, 128)]
-    share = wide[:, 0:kd]
-    for q in range(1, pack):
-        share = jnp.where(lax.rem(j, pack) == q, wide[:, q * kd:(q + 1) * kd], share)
-
     dest = None
+    a_target = d_target = share = None
     for sweep in range(SWEEPS):
         if sweep > 0:
             def row_body(q, _):
@@ -202,15 +203,19 @@
             pick = onehot(iota((8, 128), 0) == h)
             for part in split(acc[h], 2):
                 rows_sum = rows_sum + nt(pick, part)
-        gathered("dst", rows_sum, rbuf.at[sweep], s_row.at[sweep], r_row.at[sweep])()
-        anchor = rsum[...] / summed(rbuf.at[sweep], B)
-        parts = split(anchor, 3)
-        acol[:, 0:8] = nt(eye, parts[0]) + nt(eye, parts[1]) + nt(eye, parts[2])
-        if sweep == SWEEPS - 1:
-            for q in range(A):
-                asnd[q] = nn(parts[0], pa[q]) + nn(parts[1], pa[q]) + nn(parts[2], pa[q])
-            abuf[i] = asnd[i]
-            end_a = exchange("org", lambda peer: asnd.at[peer], abuf, s_a, r_a)
+        end_row = gathered("dst", rows_sum, rbuf.at[sweep], s_row.at[sweep], r_row.at[sweep])
+        if sweep == 0:
+            end_ta()
+            a_target = to_slots(ta, pa, A)
+            end_td()
+            d_target = to_slots(td, pd, B)
+            share_copy.wait()
+            share = share_in[:, 0:kd]
+            for q in range(1, pack):
+                share = jnp.where(lax.rem(j, pack) == q, share_in[:, q * kd:(q + 1) * kd], share)
+        end_row()
+        anchor = a_target / summed(rbuf.at[sweep], B)
+        acol[:, 0:8] = anchor.T
         colacc[...] = jnp.zeros_like(colacc)
 
         def col_body(q, _):
@@ -230,14 +235,15 @@
         lax.fori_loop(0, gd // CH, col_body, 0)
         cols_sum = jnp.concatenate(
             [jnp.sum(colacc[h], axis=0, keepdims=True) for h in range(hours)], axis=0)
-        gathered("org", cols_sum, cbuf.at[sweep], s_col.at[sweep], r_col.at[sweep])()
-        dest = csum[...] / summed(cbuf.at[sweep], A)
+        end_col = gathered("org", cols_sum, cbuf.at[sweep], s_col.at[sweep], r_col.at[sweep])
         if sweep == SWEEPS - 1:
-            parts = split(dest, 3)
-            for q in range(B):
-                bsnd[q] = nn(parts[0], pd[q]) + nn(parts[1], pd[q]) + nn(parts[2], pd[q])
-            bbuf[j] = bsnd[j]
-            end_b = exchange("dst", lambda peer: bsnd.at[peer], bbuf, s_b, r_b)
+            parts = stacked(anchor, 3)
+            for q in range(A):
+                asnd[q] = rows_added(nn(parts, pa[q]))
+            abuf[i] = asnd[i]
+            end_a = exchange("org", lambda peer: asnd.at[peer], abuf, s_a, r_a)
+        end_col()
+        dest = d_target / summed(cbuf.at[sweep], A)
 
         def total_body(q, _):
             rows = pl.ds(pl.multiple_of(q * CH, CH), CH)
@@ -282,23 +288,26 @@
     spread_x(j)
     to_core(i, j, 0)
 
+    parts = stacked(dest, 3)
+    for q in range(B):
+        bsnd[q] = rows_added(nn(parts, pd[q]))
+    bbuf[j] = bsnd[j]
+    end_b = exchange("dst", lambda peer: bsnd.at[peer], bbuf, s_b, r_b)
+
     o = iota((N, N), 0)
     half = N // TB // 2
     r_of = lax.div(o, 2 * half)
     e_of = lax.rem(lax.div(o, half), 2)
     p_of = lax.rem(o, half)
     order = onehot(iota((N, N), 1) == (2 * p_of + e_of) * TB + r_of)
-    own = jnp.zeros((N, 8), F32)
-    for part in split(geo_a, 3):
-        own = own + nt(order, part)
+    own = cols_added(nt(order, stacked(geo_a, 3)))
     end_a()
     end_b()
     a_own = summed(abuf, A)
     b_own = summed(bbuf, B)
     a_out[...] = a_own
     b_out[...] = b_own
-    parts = split(a_own, 3)
-    acol[:, 0:8] = nt(order, parts[0]) + nt(order, parts[1]) + nt(order, parts[2])
+    acol[:, 0:8] = cols_added(nt(order, stacked(a_own, 3)))
     acol[:, 8:16] = own
     ex, ey = dc_ref[0:1, :], dc_ref[1:2, :]
 
@@ -314,19 +323,26 @@
         remote(pfb.at[g, b], pfb.at[g, b], s_p1.at[0], sem, sib, j).wait_recv()
 
     steps = N // CH
-    lax.fori_loop(0, steps // 2, flow_body, 0)
     for k in range(1, B):
         b = lax.rem(j + k, B)
         recv(i, b, r_p1.at[b])
         spread_x(b)
         to_core(i, b, 0)
-    lax.fori_loop(steps // 2, steps, flow_body, 0)
+    lax.fori_loop(0, steps // 2, flow_body, 0)
     for k in range(1, X):
         g = lax.rem(i + A - 2 * k, A)
         for m in range(B):
             b = lax.rem(j + m, B)
             recv(g, b, r_px.at[k - 1, b])
             to_core(g, b, k)
+    lax.fori_loop(steps // 2, steps, flow_body, 0)
+    even = catch_ref[pl.ds(0, half, stride=2), :]
+    odd = catch_ref[pl.ds(1, half, stride=2), :]
+    catch = jnp.concatenate([even, odd], axis=1)
+    catch_top = lax.div(catch, 128)
+    catch_low = catch - catch_top * 128
+    for p in range(half):
+        by_low[:, p * 128:(p + 1) * 128] = onehot(iota((128, 128), 0) == catch_low[p:p + 1, :])
     left = onehot(own[:, 2:3].astype(jnp.int32) == iota((N, districts), 1))
     right = onehot(iota((districts, N), 0) == dd_ref[...])
     for k in range(X):
@@ -341,9 +357,10 @@
         for q in range(pack):
             full[g * gd + q * ph:g * gd + (q + 1) * ph, :] = jnp.concatenate(
                 [pfb[g, b, :, q * kd:(q + 1) * kd] for b in range(B)], axis=1)
-    pf_out[...] = full[...]
+    pf_copy = pltpu.make_async_copy(full, pf_out, s_pf)
+    pf_copy.start()
     high, low = split(full[...], 2)
-    full[...] = nn(nn(left, high).astype(BF16), right) + nn(nn(left, low).astype(BF16), right)
+    mixed[...] = nn(nn(left, high).astype(BF16), right) + nn(nn(left, low).astype(BF16), right)
 
     tiles = N // TB
 
@@ -353,38 +370,28 @@
             t = None
             for r in range(TB):
                 rows = pl.ds(at + r * tiles, 16)
-                term = seed[h, rows, :] * full[rows, :]
+                term = seed[h, rows, :] * mixed[rows, :]
                 t = term if t is None else t + term
-            acc[h, pl.ds(at, 16), :] = t[:, 0:128]
-            for q in range(1, N // 128):
-                acc[h, pl.ds(at + q * tiles, 16), :] = t[:, q * 128:(q + 1) * 128]
+            u[h, pl.ds(at, 16), :] = t
         return 0
 
     lax.fori_loop(0, tiles // 16, tile_body, 0)
-    for h in range(hours):
-        pair_sum = jnp.zeros((half, 128), F32)
-        for q in range(N // 128):
-            for e in range(2):
-                at = q * tiles + e * half
-                pool = onehot(lax.div(iota((128, 128), 0), TB) + q * (128 // TB) + e * tiles
-                              == iota((128, 128), 1))
-                for part in split(acc[h, at:at + half, :], 2):
-                    pair_sum = pair_sum + nn(part, pool)
-        tsum[h] = pair_sum
+    pair_sum = jnp.zeros((hours * half, 128), F32)
+    for e in range(2):
+        pool = onehot(lax.div(iota((N, 128), 0), TB) + e * tiles == iota((N, 128), 1))
+        for part in split(u[:, e * half:(e + 1) * half, :].reshape(hours * half, N), 2):
+            pair_sum = pair_sum + nn(part, pool)
+    tsum[...] = pair_sum.reshape(hours, half, 128)
 
     slabs = lanes.shape[0]
-    result = jnp.zeros((slabs * 8, 128), F32)
     slab_of = lax.div(iota((slabs * 8, 128), 0), 8)
     for p in range(half):
-        ids = catch_ref[p:p + 1, :]
-        top = lax.div(ids, 128)
-        low_of = ids - top * 128
-        t = tsum[:, p, :]
-        t = jnp.concatenate([t] * slabs, axis=0)
-        t = jnp.where(slab_of == top, t, 0.0)
-        lo = onehot(iota((128, 128), 0) == low_of)
-        for part in split(t, 2):
-            result = result + nt(part, lo)
+        t = jnp.concatenate([tsum[:, p, :]] * slabs, axis=0)
+        t = jnp.where(slab_of == catch_top[p:p + 1, :], t, 0.0)
+        for m, part in enumerate(split(t, 2)):
+            by_slab[m * slabs * 8:(m + 1) * slabs * 8, p * 128:(p + 1) * 128] = part
+    result = nt(by_slab[...], by_low[...])
+    result = result[0:slabs * 8] + result[slabs * 8:]
     lanes[...] = result.reshape(slabs, 8, 128)
 
     per = slabs // A
@@ -400,6 +407,7 @@
         mine = jnp.where(lax.rem(j, share_of) == q,
                          total[:, q * LANE_DEV:(q + 1) * LANE_DEV], mine)
     lane_out[...] = mine
+    pf_copy.wait()
 
 
 def per_device(
@@ -421,12 +429,13 @@
         V((A, N, N), BF16), V((B, N, N), BF16),
         V((hours, N, N), F32), V((hours, N, 128), F32), V((hours, gd, N), F32),
         V((gd, N), F32), V((N, 128), F32), V((hours, 8, N), F32),
-        V((8, N), F32), V((8, N), F32),
         V((SWEEPS, B, 8, N), F32), V((SWEEPS, A, 8, N), F32),
         V((A, 8, N), F32), V((B, 8, N), F32), V((A, 8, N), F32), V((B, 8, N), F32),
-        V((A, B, ph, 128), F32), V((districts, districts), F32),
+        V((A, B, ph, 128), F32), V((districts, districts), F32), V((N, N), F32),
         V((hours, N // TB // 2, 128), F32), V((slabs, 8, 128), F32),
         V((A, slabs // A, 8, 128), F32), V((slabs // A, 8, 128), F32), V((B, 8, 128), F32),
+        V((gd, 128), F32), V((slabs * 16, N // TB * (N // TB)), BF16),
+        V((128, N // TB * (N // TB)), BF16), dma(()), dma(()),
     ]
     X = A // 2
     for shape in (
@@ -438,6 +447,7 @@
     ):
         scratch.append(dma(shape))
     vm = pl.BlockSpec(memory_space=pltpu.VMEM)
+    anywhere = pl.BlockSpec(memory_space=pl.ANY)
     return tuple(pl.pallas_call(
         functools.partial(kernel, A, B),
         out_shape=(
@@ -446,8 +456,8 @@
             jax.ShapeDtypeStruct((hours, N), F32),
             jax.ShapeDtypeStruct((hours, LANE_DEV), F32),
         ),
-        in_specs=[pl.BlockSpec(memory_space=pltpu.SMEM)] + [vm] * 8,
-        out_specs=(vm, vm, vm, vm),
+        in_specs=[pl.BlockSpec(memory_space=pltpu.SMEM)] + [vm] * 6 + [anywhere, vm],
+        out_specs=(anywhere, vm, vm, vm),
         scratch_shapes=scratch,
         compiler_params=pltpu.CompilerParams(
             collective_id=0, has_side_effects=True, vmem_limit_bytes=56 * 1024 * 1024),
@@ -455,7 +465,7 @@
         hour_decay, anchor_coords, dest_coords,
         anchor_district.reshape(1, N), dest_district.reshape(1, N),
         anchor_target, dest_target, pair_share,
-        catchment.reshape(N // TB // 2, 128),
+        catchment,
     ))
 
 

time: 98.4 us -> 77.1 us (0.78)
  Pallas kernels: 91.8 us -> 71.9 us
  local copies, waits for them, and re-layouts: 5.7 us -> 4.26 us
    pallas_call x1, Pallas kernels: 91.8 us -> 71.9 us  [per_device(): pl.pallas_call(functools.partial(kernel, A, B), out_shape=(jax.ShapeDtype...]
    reshape x1 -> x0, local copies, waits for them, and re-layouts: 1.43 us -> none  [per_device(): catchment.reshape(N // TB // 2, 128)]
where the time goes in v2:
time: 77.1 us; the launch traced here: 76.8 us
  Pallas kernels  71.9 us (93%)
  local copies, waits for them, and re-layouts  4.26 us (6%)
    pallas_call x1, Pallas kernels, per_device(): pl.pallas_call(functools.partial(kernel, A, B), out_shape=(jax.ShapeDtype...  71.9 us
    unnamed x10, local copies, waits for them, and re-layouts  4.26 us

profile of v2, /device:TPU:0, one launch (start us, length us, event | category | flops | bytes accessed | tf_op | source)
XLA Modules:
  0.0 76.8 jit_solution(4400557457721191124)
XLA Ops:
  0.6 71.9 %shard_map.120 = (f32[512,512]{1,0:T(8,128)}, f32[8,512]{1,0:T(8,128)}, f32[8,512]{1,0:T(8,128)}, f32[8,32]{1,0:T(8,128)}) custom-call(f32[8]{0:T(128)} %decay_ref.1, f32[2,512]{1,0:T(2,128)} %ac_ref.1, f32[2,512]{1,0:T(2,128)} %dc_ref.1, s32[1,512]{1,0:T(1,128)} %bitcast.2, s32[1,512]{1,0:T(1,128)} %bitcast.3, f32[8,512]{1,0:T(8,128)} %at_ref.1, ...), custom_call_target="tpu_custom_call" | custom-call | tf_op jit(solution)/shard_map/pallas_call | solution.py:451
  72.5 0.0 copy-start.1
  72.5 2.3 %copy.17 = f32[512,512]{1,0:T(8,128)} copy(f32[512,512]{1,0:T(8,128)} %get-tuple-element.8) | data formatting | bytes 2097152
  74.8 0.0 copy-done.1
  74.8 0.0 copy-start
  74.8 0.6 copy.18
  75.4 0.1 copy-done
  75.5 0.0 copy-start.2
  75.5 0.6 copy.19
  76.1 0.1 copy-done.2
  76.2 0.6 copy.20
Async XLA Ops:
  72.5 2.3 %copy-start.1 = (f32[8,512]{1,0:T(8,128)S(1)}, f32[8,512]{1,0:T(8,128)}, u32[]{:S(2)}) copy-start(f32[8,512]{1,0:T(8,128)} %get-tuple-element.9) | copy-start | bytes 49156
  74.8 0.7 copy-start
  75.5 0.7 copy-start.2
